TPU v7x, 512 devices: a whole 4x4x16 slice. The times are simulated.
512 devices in a mesh: dp: 4 (over z_lo), expert: 128 (over y, x, z_hi, core).
Axes of the slice: x: 4, y: 4, z: 16 (z_hi: 4, z_lo: 4; z = z_hi * 4 + z_lo), core: 2. Of those that a mesh axis runs over, the one named last changes fastest.
Arguments:
- hidden_in: bfloat16 [2, 8192, 2048], P(None, ('dp', 'expert')), may hold values from -6 to 6
- cotangent: bfloat16 [2, 8192, 2048], P(None, ('dp', 'expert')), may hold values from -6 to 6
- expert_ids: int32 [2, 8192, 8], P(None, ('dp', 'expert')), may hold values from 0 to 127, all different within a row; in each aligned block of 16 rows (0 to 15, 16 to 31, ..., all dimensions but the last counted through in order) at most 2 rows name the same one
- route_prob: float32 [2, 8192, 8], P(None, ('dp', 'expert')), may hold values from 0.05 to 1
- swap_flags: int32 [64], replicated, may hold values 0 or 1
- gate_up: bfloat16 [128, 2048, 2, 384], P('expert', 'dp'), may hold values from -0.125 to 0.125
- down_t: bfloat16 [128, 2048, 384], P('expert', 'dp'), may hold values from -0.3125 to 0.3125
Outputs:
- hidden_out: bfloat16 [2, 8192, 2048], P(None, ('dp', 'expert'))
- input_grad: bfloat16 [2, 8192, 2048], P(None, ('dp', 'expert'))
- resident_gate_up: bfloat16 [128, 2048, 2, 384], P('expert', 'dp')
- resident_down: bfloat16 [128, 2048, 384], P('expert', 'dp')
Inputs may be any that keep to these rules, and one draw needn't show every extreme that they name: `expert_ids`: within one microbatch the 16 tokens of one device name any one expert at most 2 times, a bound that some block reaches.
All inputs are finite; a program needn't handle non-finite values.
Results may differ from a plain program's by a relative error of at most 0.0064.
Values may be sent and summed in bfloat16 or wider, within the bound.
No kernel may reach another device: no remote copies, remote signals or barrier semaphores. Data moves between devices by JAX's collectives and lax.ppermute only.
A program may use at most 64 MiB of HBM per device.

v0:
```python
import jax
import jax.numpy as jnp
from jax import lax
from jax.sharding import Mesh, PartitionSpec as P

EXPERT = ("y", "x", "z", "c")
PLANE = ("y", "x", "c")
BF = jnp.bfloat16
F32 = jnp.float32


def along_z(value, shift):
    count = lax.axis_size("z")
    return lax.ppermute(value, "z", [(i, (i + shift) % count) for i in range(count)])


def local(hidden_in, cotangent, expert_ids, route_prob, swap_flags, gate_up, down_t):
    micro, tok, width = hidden_in.shape
    top = expert_ids.shape[2]
    hid = down_t.shape[2]
    nz = lax.axis_size("z")
    ny = lax.axis_size("y")
    plane = ny * lax.axis_size("x") * 2
    my_z = lax.axis_index("z")
    my_y = lax.axis_index("y")
    half = ny * lax.axis_size("x") * nz
    my_index = lax.axis_index(EXPERT)
    flag = jnp.sum(jnp.where(jnp.arange(half, dtype=jnp.int32) == my_index % half, swap_flags, 0))
    pairs = [(i, i ^ ny // 2) for i in range(ny)]
    other_gate = lax.ppermute(gate_up, "y", pairs)
    other_down = lax.ppermute(down_t, "y", pairs)
    resident_gate = jnp.where(flag == 1, other_gate, gate_up)
    resident_down = jnp.where(flag == 1, other_down, down_t)
    mine = jnp.stack([hidden_in, cotangent])
    facts = jnp.concatenate([expert_ids.astype(F32), route_prob], axis=2)
    facts = jnp.stack([facts] + [along_z(facts, s) for s in range(1, nz)])
    column = jnp.stack([mine] + [along_z(mine, s) for s in range(1, nz)])
    weights = jnp.concatenate([gate_up.reshape(-1, 2 * hid), down_t.reshape(-1, hid)], axis=1)
    weights = lax.all_gather(weights, "dp", axis=0, tiled=True)
    gate_matrix = weights[:, : 2 * hid]
    down_matrix = weights[:, 2 * hid :]
    ids = facts[..., :top].astype(jnp.int32)
    prob = facts[..., top:]
    core = ids % 2
    place = ids // (2 * nz) * 2 + core
    place = jnp.where(ids // 2 % nz == my_z, place, -1)
    hit = place[..., None] == jnp.arange(plane, dtype=jnp.int32)
    member = jnp.any(hit, axis=3)
    weight = jnp.sum(jnp.where(hit, prob[..., None], 0.0), axis=3)
    below = jnp.tril(jnp.ones((tok, tok), F32), -1)
    earlier = jnp.einsum("ut,smtd->smud", below, member.astype(F32))
    rank = jnp.arange(2, dtype=jnp.int32).astype(F32)
    pick = member[..., None] & (earlier[..., None] == rank)
    pick = pick.astype(F32)
    slot_weight = jnp.einsum("smtdr,smtd->dmsr", pick, weight)
    pick_b = pick.astype(BF)
    rows_x = jnp.einsum(
        "smtdr,smtw->dmsrw", pick_b, column[:, 0], preferred_element_type=F32
    ).astype(BF)
    rows_g = jnp.einsum("smtdr,smtw->dmsrw", pick_b, column[:, 1], preferred_element_type=F32)
    rows_g = (rows_g * slot_weight[..., None]).astype(BF)
    count = micro * nz * 2
    rows = jnp.concatenate(
        [rows_x.reshape(plane, count, width), rows_g.reshape(plane, count, width)], axis=1
    )
    rows = lax.all_to_all(rows, PLANE, 0, 0, tiled=True)
    tokens_now = rows[:, :count].reshape(plane * count, width)
    grads_now = rows[:, count:].reshape(plane * count, width)
    projected = jnp.dot(tokens_now, gate_matrix, preferred_element_type=F32)
    gate_part = projected[:, :hid]
    upper_part = projected[:, hid:]
    sig = jax.nn.sigmoid(gate_part)
    hidden = (gate_part * sig * upper_part).astype(BF)
    last = (((1,), (1,)), ((), ()))
    expert_out = lax.dot_general(hidden, down_matrix, last, preferred_element_type=F32).astype(BF)
    d_hidden = jnp.dot(grads_now, down_matrix, preferred_element_type=F32)
    d_gate = (d_hidden * upper_part * sig * (1.0 + gate_part * (1.0 - sig))).astype(BF)
    d_upper = (d_hidden * gate_part * sig).astype(BF)
    d_joined = jnp.concatenate([d_gate, d_upper], axis=1)
    row_input = lax.dot_general(d_joined, gate_matrix, last, preferred_element_type=F32).astype(BF)
    back = jnp.concatenate(
        [expert_out.reshape(plane, count, width), row_input.reshape(plane, count, width)], axis=1
    )
    back = lax.all_to_all(back, PLANE, 0, 0, tiled=True)
    back_out = back[:, :count].reshape(plane, micro, nz, 2, width)
    back_grad = back[:, count:].reshape(plane, micro, nz, 2, width)
    scaled = pick * weight[..., None]
    scaled_high = scaled.astype(BF)
    scaled_low = (scaled - scaled_high.astype(F32)).astype(BF)
    form = "smtdr,dmsrw->smtw"
    part_out = jnp.einsum(form, scaled_high, back_out, preferred_element_type=F32) + jnp.einsum(
        form, scaled_low, back_out, preferred_element_type=F32
    )
    part_grad = jnp.einsum(form, pick_b, back_grad, preferred_element_type=F32)
    part = jnp.stack([part_out, part_grad], axis=1)
    total = part[0]
    for s in range(1, nz):
        total = total + along_z(part[s].astype(BF), -s).astype(F32)
    total = total.astype(BF)
    return (total[0], total[1], resident_gate, resident_down)


def solution(mesh):
    devices = mesh.devices.reshape(4, 4, 4, 4, 2)
    fine = Mesh(devices, ("dp", "y", "x", "z", "c"))
    tokens = P(None, ("dp",) + EXPERT, None)
    placed = (
        tokens,
        tokens,
        tokens,
        tokens,
        P(),
        P(EXPERT, "dp", None, None),
        P(EXPERT, "dp", None),
    )
    return jax.shard_map(
        local,
        mesh=fine,
        in_specs=placed,
        out_specs=(tokens, tokens, P(EXPERT, "dp", None, None), P(EXPERT, "dp", None)),
        check_vma=False,
    )
```

profile of v0, /device:TPU:117, one launch (start us, length us, event | category | flops | bytes accessed | tf_op | source)
XLA Modules:
  0.0 333.7 jit_solution(6145874898485073797)
XLA Ops:
  7.2 0.7 convert_element_type.77
  7.9 0.7 fusion.60
  8.6 8.8 %collective-permute-start = (f32[2,16,16]{1,2,0:T(8,128)S(1)}, f32[2,16,16]{1,2,0:T(8,128)S(1)}, u32[]{:S(2)}, u32[]{:S(2)}) collective-permute-start(f32[2,16,16]{1,2,0:T(8,128)S(1)} %get-tuple-element.18), channel_id=1, source_target_pairs={{0,2},{2,4},{4,6},{6,0},{1,3},{3,5},{5,7},{7,1},{8,10},{10,12},{12... | collective-permute-start | bytes 6152 | tf_op jit(solution)/shard_map/ppermute | solution.py:14
  17.4 7.9 %collective-permute-start.1 = (f32[2,16,16]{1,2,0:T(8,128)S(1)}, f32[2,16,16]{1,2,0:T(8,128)S(1)}, u32[]{:S(2)}, u32[]{:S(2)}) collective-permute-start(f32[2,16,16]{1,2,0:T(8,128)S(1)} %get-tuple-element.18), channel_id=1, source_target_pairs={{0,4},{2,6},{4,0},{6,2},{1,5},{3,7},{5,1},{7,3},{8,12},{10,14},{12... | collective-permute-start | bytes 6152 | tf_op jit(solution)/shard_map/ppermute | solution.py:14
  25.4 5.2 %collective-permute-start.2 = (f32[2,16,16]{1,2,0:T(8,128)S(1)}, f32[2,16,16]{1,2,0:T(8,128)S(1)}, u32[]{:S(2)}, u32[]{:S(2)}) collective-permute-start(f32[2,16,16]{1,2,0:T(8,128)S(1)} %get-tuple-element.18), channel_id=1, source_target_pairs={{0,6},{2,0},{4,2},{6,4},{1,7},{3,1},{5,3},{7,5},{8,14},{10,8},{12,... | collective-permute-start | bytes 6152 | tf_op jit(solution)/shard_map/ppermute | solution.py:14
  30.6 1.3 copy.101
  31.8 2.1 pad_maximum_fusion.3
  34.1 4.0 %collective-permute-start.3 = (bf16[2,2,16,2048]{3,2,1,0:T(8,128)(2,1)S(1)}, bf16[2,2,16,2048]{3,2,1,0:T(8,128)(2,1)S(1)}, u32[]{:S(2)}, u32[]{:S(2)}) collective-permute-start(bf16[2,2,16,2048]{3,2,1,0:T(8,128)(2,1)S(1)} %get-tuple-element.16), channel_id=1, source_target_pairs={{0,2},{2,4},{4,6},{6,0},{1,3},{3,5},{5,7},{7,1},{8,10},{10,12},{12... | collective-permute-start | bytes 786440 | tf_op jit(solution)/shard_map/ppermute | solution.py:14
  38.1 6.1 %collective-permute-start.4 = (bf16[2,2,16,2048]{3,2,1,0:T(8,128)(2,1)S(1)}, bf16[2,2,16,2048]{3,2,1,0:T(8,128)(2,1)S(1)}, u32[]{:S(2)}, u32[]{:S(2)}) collective-permute-start(bf16[2,2,16,2048]{3,2,1,0:T(8,128)(2,1)S(1)} %get-tuple-element.16), channel_id=1, source_target_pairs={{0,4},{2,6},{4,0},{6,2},{1,5},{3,7},{5,1},{7,3},{8,12},{10,14},{12... | collective-permute-start | bytes 786440 | tf_op jit(solution)/shard_map/ppermute | solution.py:14
  44.2 2.9 collective-permute-start.5
  47.3 0.3 fusion.22
  47.8 0.3 select_reduce_fusion
  48.3 14.5 %collective-permute-done.3 = bf16[2,2,16,2048]{3,2,1,0:T(8,128)(2,1)S(1)} collective-permute-done((bf16[2,2,16,2048]{3,2,1,0:T(8,128)(2,1)S(1)}, bf16[2,2,16,2048]{3,2,1,0:T(8,128)(2,1)S(1)}, u32[]{:S(2)}, u32[]{:S(2)}) %collective-permute-start.3) | collective-permute-done | bytes 262176 | tf_op jit(solution)/shard_map/ppermute | solution.py:14
  62.8 11.7 %collective-permute-done.4 = bf16[2,2,16,2048]{3,2,1,0:T(8,128)(2,1)S(1)} collective-permute-done((bf16[2,2,16,2048]{3,2,1,0:T(8,128)(2,1)S(1)}, bf16[2,2,16,2048]{3,2,1,0:T(8,128)(2,1)S(1)}, u32[]{:S(2)}, u32[]{:S(2)}) %collective-permute-start.4) | collective-permute-done | bytes 262176 | tf_op jit(solution)/shard_map/ppermute | solution.py:14
  74.5 16.0 %collective-permute-done.5 = bf16[2,2,16,2048]{3,2,1,0:T(8,128)(2,1)S(1)} collective-permute-done((bf16[2,2,16,2048]{3,2,1,0:T(8,128)(2,1)S(1)}, bf16[2,2,16,2048]{3,2,1,0:T(8,128)(2,1)S(1)}, u32[]{:S(2)}, u32[]{:S(2)}) %collective-permute-start.5) | collective-permute-done | bytes 262176 | tf_op jit(solution)/shard_map/ppermute | solution.py:14
  90.6 0.8 fusion
  91.5 1.2 copy.69
  92.6 0.8 convolution_convert_fusion.2
  93.5 1.2 copy.68
  94.6 0.6 pad_maximum_fusion
  95.2 59.0 %all_to_all.10 = bf16[32,32,2048]{2,1,0:T(8,128)(2,1)S(1)} all-to-all(bf16[32,32,2048]{2,1,0:T(8,128)(2,1)S(1)} %pad_maximum_fusion), channel_id=1, replica_groups=mesh['dp'=4,'y'=4,'x'=4,'z'=4,'c'=2] {'y','x','c'}, dimensions={0} | all-to-all | bytes 8388608 | tf_op jit(solution)/shard_map/all_to_all | solution.py:66
  154.2 1.8 fusion.63
  155.9 10.1 %all-gather.2.cloned.1.call-done = bf16[2048,1152]{1,0:T(8,128)(2,1)} async-done(((bf16[512,1152]{1,0:T(8,128)(2,1)}), bf16[2048,1152]{1,0:T(8,128)(2,1)}) %all-gather.2.cloned.1.call-update) | async-done | bytes 4718608 | tf_op jit(solution)/shard_map/all_gather | solution.py:39
  166.0 4.5 %fusion.2 = f32[512,768]{1,0:T(8,128)S(1)} fusion(bf16[512,2048]{1,0:T(8,128)(2,1)} %bitcast.117, bf16[2048,1152]{1,0:T(8,128)(2,1)} %all-gather.2.cloned.1.call-done), kind=kOutput, calls=%fused_computation.8 | convolution fusion | flops 1610612736 | bytes 6815744 | tf_op jit(solution)/shard_map/dot_general | solution.py:69
  170.5 1.3 convolution_convert_fusion.1
  171.8 1.4 multiply_convert_fusion.1
  173.3 1.8 convolution_convert_fusion
  175.1 2.6 pad_maximum_fusion.1
  177.7 7.8 %all-to-all-start.1 = ((bf16[32,32,2048]{2,1,0:T(8,128)(2,1)}), bf16[32,32,2048]{2,1,0:T(8,128)(2,1)}, u32[]{:S(2)}, u32[]{:S(2)}) async-start(bf16[32,32,2048]{2,1,0:T(8,128)(2,1)} %pad_maximum_fusion.1), calls=%async_computation.1 | async-start | bytes 8388608 | tf_op jit(solution)/shard_map/all_to_all | solution.py:84
  185.5 2.2 collective-permute-start.10
  187.7 4.6 %collective-permute-start.9 = (bf16[1,512,2,384]{3,2,1,0:T(2,128)(2,1)S(1)}, bf16[1,512,2,384]{3,2,1,0:T(2,128)(2,1)S(1)}, u32[]{:S(2)}, u32[]{:S(2)}) collective-permute-start(bf16[1,512,2,384]{3,2,1,0:T(2,128)(2,1)S(1)} %copy-done), channel_id=1, source_target_pairs={{0,64},{32,96},{64,0},{96,32},{1,65},{33,97},{65,1},{97,33},{2,66}... | collective-permute-start | bytes 2359304 | tf_op jit(solution)/shard_map/ppermute | solution.py:30
  192.3 0.6 fusion.53
  193.6 46.3 %collective-permute-done.10 = bf16[1,512,384]{2,1,0:T(8,128)(2,1)S(1)} collective-permute-done((bf16[1,512,384]{2,1,0:T(8,128)(2,1)S(1)}, bf16[1,512,384]{2,1,0:T(8,128)(2,1)S(1)}, u32[]{:S(2)}, u32[]{:S(2)}) %collective-permute-start.10) | collective-permute-done | bytes 393248 | tf_op jit(solution)/shard_map/ppermute | solution.py:31
  239.9 0.8 broadcast_select_fusion.1
  240.7 16.6 %all-to-all-done.1 = bf16[32,32,2048]{2,1,0:T(8,128)(2,1)} async-done(((bf16[32,32,2048]{2,1,0:T(8,128)(2,1)}), bf16[32,32,2048]{2,1,0:T(8,128)(2,1)}, u32[]{:S(2)}, u32[]{:S(2)}) %all-to-all-start.1) | async-done | bytes 4194336 | tf_op jit(solution)/shard_map/all_to_all | solution.py:84
  257.3 2.7 fusion.62
  260.1 1.2 copy.95
  261.2 0.5 convolution_bitcast_fusion.2
  261.7 1.2 copy.96
  262.9 0.5 convolution_bitcast_fusion
  263.4 0.5 fusion.5
  264.2 2.7 collective-permute-start.6
  266.9 10.3 %collective-permute-start.7 = (bf16[2,2,16,2048]{3,2,1,0:T(8,128)(2,1)S(1)}, bf16[2,2,16,2048]{3,2,1,0:T(8,128)(2,1)S(1)}, u32[]{:S(2)}, u32[]{:S(2)}) collective-permute-start(bf16[2,2,16,2048]{3,2,1,0:T(8,128)(2,1)S(1)} %get-tuple-element.12), channel_id=1, source_target_pairs={{0,4},{2,6},{4,0},{6,2},{1,5},{3,7},{5,1},{7,3},{8,12},{10,14},{12... | collective-permute-start | bytes 786440 | tf_op jit(solution)/shard_map/ppermute | solution.py:14
  277.2 2.9 collective-permute-start.8
  280.2 1.0 broadcast_select_fusion
  281.1 39.5 %collective-permute-done.7 = bf16[2,2,16,2048]{3,2,1,0:T(8,128)(2,1)S(1)} collective-permute-done((bf16[2,2,16,2048]{3,2,1,0:T(8,128)(2,1)S(1)}, bf16[2,2,16,2048]{3,2,1,0:T(8,128)(2,1)S(1)}, u32[]{:S(2)}, u32[]{:S(2)}) %collective-permute-start.7) | collective-permute-done | bytes 262176 | tf_op jit(solution)/shard_map/ppermute | solution.py:14
  320.6 5.4 %collective-permute-done.8 = bf16[2,2,16,2048]{3,2,1,0:T(8,128)(2,1)S(1)} collective-permute-done((bf16[2,2,16,2048]{3,2,1,0:T(8,128)(2,1)S(1)}, bf16[2,2,16,2048]{3,2,1,0:T(8,128)(2,1)S(1)}, u32[]{:S(2)}, u32[]{:S(2)}) %collective-permute-start.8) | collective-permute-done | bytes 262176 | tf_op jit(solution)/shard_map/ppermute | solution.py:14
  326.2 0.7 slice_bitcast_fusion.7
  (33 shorter events, 1.2 us)
Async XLA Ops:
  7.2 158.9 %all-gather.2.cloned.1.call-start = ((), (), s32[]{:S(2)}) async-start(), calls=%async_computation.2 | async-start | bytes 5898240 | tf_op jit(solution)/shard_map/all_gather | solution.py:39
  8.6 35.6 %collective-permute-start = (f32[2,16,16]{1,2,0:T(8,128)S(1)}, f32[2,16,16]{1,2,0:T(8,128)S(1)}, u32[]{:S(2)}, u32[]{:S(2)}) collective-permute-start(f32[2,16,16]{1,2,0:T(8,128)S(1)} %get-tuple-element.18), channel_id=1, source_target_pairs={{0,2},{2,4},{4,6},{6,0},{1,3},{3,5},{5,7},{7,1},{8,10},{10,12},{12... | collective-permute-start | bytes 6152 | tf_op jit(solution)/shard_map/ppermute | solution.py:14
  17.4 29.7 %collective-permute-start.1 = (f32[2,16,16]{1,2,0:T(8,128)S(1)}, f32[2,16,16]{1,2,0:T(8,128)S(1)}, u32[]{:S(2)}, u32[]{:S(2)}) collective-permute-start(f32[2,16,16]{1,2,0:T(8,128)S(1)} %get-tuple-element.18), channel_id=1, source_target_pairs={{0,4},{2,6},{4,0},{6,2},{1,5},{3,7},{5,1},{7,3},{8,12},{10,14},{12... | collective-permute-start | bytes 6152 | tf_op jit(solution)/shard_map/ppermute | solution.py:14
  25.4 21.7 %collective-permute-start.2 = (f32[2,16,16]{1,2,0:T(8,128)S(1)}, f32[2,16,16]{1,2,0:T(8,128)S(1)}, u32[]{:S(2)}, u32[]{:S(2)}) collective-permute-start(f32[2,16,16]{1,2,0:T(8,128)S(1)} %get-tuple-element.18), channel_id=1, source_target_pairs={{0,6},{2,0},{4,2},{6,4},{1,7},{3,1},{5,3},{7,5},{8,14},{10,8},{12,... | collective-permute-start | bytes 6152 | tf_op jit(solution)/shard_map/ppermute | solution.py:14
  31.8 2.2 copy-start.2
  31.8 2.2 copy-start.3
  34.1 28.8 %collective-permute-start.3 = (bf16[2,2,16,2048]{3,2,1,0:T(8,128)(2,1)S(1)}, bf16[2,2,16,2048]{3,2,1,0:T(8,128)(2,1)S(1)}, u32[]{:S(2)}, u32[]{:S(2)}) collective-permute-start(bf16[2,2,16,2048]{3,2,1,0:T(8,128)(2,1)S(1)} %get-tuple-element.16), channel_id=1, source_target_pairs={{0,2},{2,4},{4,6},{6,0},{1,3},{3,5},{5,7},{7,1},{8,10},{10,12},{12... | collective-permute-start | bytes 786440 | tf_op jit(solution)/shard_map/ppermute | solution.py:14
  38.1 36.4 %collective-permute-start.4 = (bf16[2,2,16,2048]{3,2,1,0:T(8,128)(2,1)S(1)}, bf16[2,2,16,2048]{3,2,1,0:T(8,128)(2,1)S(1)}, u32[]{:S(2)}, u32[]{:S(2)}) collective-permute-start(bf16[2,2,16,2048]{3,2,1,0:T(8,128)(2,1)S(1)} %get-tuple-element.16), channel_id=1, source_target_pairs={{0,4},{2,6},{4,0},{6,2},{1,5},{3,7},{5,1},{7,3},{8,12},{10,14},{12... | collective-permute-start | bytes 786440 | tf_op jit(solution)/shard_map/ppermute | solution.py:14
  44.2 46.3 %collective-permute-start.5 = (bf16[2,2,16,2048]{3,2,1,0:T(8,128)(2,1)S(1)}, bf16[2,2,16,2048]{3,2,1,0:T(8,128)(2,1)S(1)}, u32[]{:S(2)}, u32[]{:S(2)}) collective-permute-start(bf16[2,2,16,2048]{3,2,1,0:T(8,128)(2,1)S(1)} %get-tuple-element.16), channel_id=1, source_target_pairs={{0,6},{2,0},{4,2},{6,4},{1,7},{3,1},{5,3},{7,5},{8,14},{10,8},{12,... | collective-permute-start | bytes 786440 | tf_op jit(solution)/shard_map/ppermute | solution.py:14
  166.0 4.5 %copy-start.4 = (bf16[2048,1152]{1,0:T(8,128)(2,1)S(1)}, bf16[2048,1152]{1,0:T(8,128)(2,1)}, u32[]{:S(2)}) copy-start(bf16[2048,1152]{1,0:T(8,128)(2,1)} %all-gather.2.cloned.1.call-done) | copy-start | bytes 14155780
  177.7 7.8 %copy-start.1 = (bf16[1,512,384]{2,1,0:T(8,128)(2,1)S(1)}, bf16[1,512,384]{2,1,0:T(8,128)(2,1)}, u32[]{:S(2)}) copy-start(bf16[1,512,384]{2,1,0:T(8,128)(2,1)} %param.13) | copy-start | bytes 1179652
  177.7 10.0 %copy-start = (bf16[1,512,2,384]{3,2,1,0:T(2,128)(2,1)S(1)}, bf16[1,512,2,384]{3,2,1,0:T(2,128)(2,1)}, u32[]{:S(2)}) copy-start(bf16[1,512,2,384]{3,2,1,0:T(2,128)(2,1)} %param.12) | copy-start | bytes 2359300
  177.7 14.7 %copy-start.5 = (s32[64]{0:T(128)S(1)}, s32[64]{0:T(128)}, u32[]{:S(2)}) copy-start(s32[64]{0:T(128)} %param.11) | copy-start | bytes 772
  177.7 79.6 %all-to-all-start.1 = ((bf16[32,32,2048]{2,1,0:T(8,128)(2,1)}), bf16[32,32,2048]{2,1,0:T(8,128)(2,1)}, u32[]{:S(2)}, u32[]{:S(2)}) async-start(bf16[32,32,2048]{2,1,0:T(8,128)(2,1)} %pad_maximum_fusion.1), calls=%async_computation.1 | async-start | bytes 8388608 | tf_op jit(solution)/shard_map/all_to_all | solution.py:84
  185.5 54.4 %collective-permute-start.10 = (bf16[1,512,384]{2,1,0:T(8,128)(2,1)S(1)}, bf16[1,512,384]{2,1,0:T(8,128)(2,1)S(1)}, u32[]{:S(2)}, u32[]{:S(2)}) collective-permute-start(bf16[1,512,384]{2,1,0:T(8,128)(2,1)S(1)} %copy-done.1), channel_id=1, source_target_pairs={{0,64},{32,96},{64,0},{96,32},{1,65},{33,97},{65,1},{97,33},{2,66}... | collective-permute-start | bytes 1179656 | tf_op jit(solution)/shard_map/ppermute | solution.py:31
  187.7 92.5 %collective-permute-start.9 = (bf16[1,512,2,384]{3,2,1,0:T(2,128)(2,1)S(1)}, bf16[1,512,2,384]{3,2,1,0:T(2,128)(2,1)S(1)}, u32[]{:S(2)}, u32[]{:S(2)}) collective-permute-start(bf16[1,512,2,384]{3,2,1,0:T(2,128)(2,1)S(1)} %copy-done), channel_id=1, source_target_pairs={{0,64},{32,96},{64,0},{96,32},{1,65},{33,97},{65,1},{97,33},{2,66}... | collective-permute-start | bytes 2359304 | tf_op jit(solution)/shard_map/ppermute | solution.py:30
  264.2 16.9 %collective-permute-start.6 = (bf16[2,2,16,2048]{3,2,1,0:T(8,128)(2,1)S(1)}, bf16[2,2,16,2048]{3,2,1,0:T(8,128)(2,1)S(1)}, u32[]{:S(2)}, u32[]{:S(2)}) collective-permute-start(bf16[2,2,16,2048]{3,2,1,0:T(8,128)(2,1)S(1)} %get-tuple-element.10), channel_id=1, source_target_pairs={{0,6},{2,0},{4,2},{6,4},{1,7},{3,1},{5,3},{7,5},{8,14},{10,8},{12,... | collective-permute-start | bytes 786440 | tf_op jit(solution)/shard_map/ppermute | solution.py:14
  266.9 53.8 %collective-permute-start.7 = (bf16[2,2,16,2048]{3,2,1,0:T(8,128)(2,1)S(1)}, bf16[2,2,16,2048]{3,2,1,0:T(8,128)(2,1)S(1)}, u32[]{:S(2)}, u32[]{:S(2)}) collective-permute-start(bf16[2,2,16,2048]{3,2,1,0:T(8,128)(2,1)S(1)} %get-tuple-element.12), channel_id=1, source_target_pairs={{0,4},{2,6},{4,0},{6,2},{1,5},{3,7},{5,1},{7,3},{8,12},{10,14},{12... | collective-permute-start | bytes 786440 | tf_op jit(solution)/shard_map/ppermute | solution.py:14
  277.2 48.8 %collective-permute-start.8 = (bf16[2,2,16,2048]{3,2,1,0:T(8,128)(2,1)S(1)}, bf16[2,2,16,2048]{3,2,1,0:T(8,128)(2,1)S(1)}, u32[]{:S(2)}, u32[]{:S(2)}) collective-permute-start(bf16[2,2,16,2048]{3,2,1,0:T(8,128)(2,1)S(1)} %get-tuple-element.11), channel_id=1, source_target_pairs={{0,2},{2,4},{4,6},{6,0},{1,3},{3,5},{5,7},{7,1},{8,10},{10,12},{12... | collective-permute-start | bytes 786440 | tf_op jit(solution)/shard_map/ppermute | solution.py:14
Sparse Core Ops, SparseCore 0:
  34.1 131.8 all-gather.1
where the time goes:
time: 334 us
  waiting for transfers between devices  160 us (48%)
  starting transfers between devices  65.4 us (20%)
  blocking collectives  59 us (18%)
  between operations  15.1 us (5%)
  matrix products  12.4 us (4%)
  local copies, waits for them, and re-layouts  11.4 us (3%)
  other arithmetic  10.4 us (3%)
    ppermute x9, waiting for transfers between devices, along_z(): lax.ppermute(value, 'z', [(i, (i + shift) % count) for i in range(count)])  87.1 us
    all_to_all x1, blocking collectives, local(): rows = lax.all_to_all(rows, PLANE, 0, 0, tiled=True)  59 us
    ppermute x9, starting transfers between devices, along_z(): lax.ppermute(value, 'z', [(i, (i + shift) % count) for i in range(count)])  50.8 us
    ppermute x1, waiting for transfers between devices, local(): other_down = lax.ppermute(down_t, 'y', pairs)  46.3 us
    all_to_all x1, waiting for transfers between devices, local(): back = lax.all_to_all(back, PLANE, 0, 0, tiled=True)  16.6 us
    all_gather x1, waiting for transfers between devices, local(): weights = lax.all_gather(weights, 'dp', axis=0, tiled=True)  10.1 us
    all_to_all x1, starting transfers between devices, local(): back = lax.all_to_all(back, PLANE, 0, 0, tiled=True)  7.81 us
  transfers between devices with their start and end apart: 13, of which 8 were waited for; matrix products, arithmetic and copies ran while one was open for 6% of the time, Pallas kernels for 0%

commit v1 on v0

--- a/solution.py
+++ b/solution.py
@@ -7,6 +7,13 @@
 PLANE = ("y", "x", "c")
 BF = jnp.bfloat16
 F32 = jnp.float32
+
+
+def exchange_gather(x, axis, along):
+    count = lax.axis_size(axis)
+    blocks = jnp.stack([x for _ in range(count)])
+    blocks = lax.all_to_all(blocks, axis, split_axis=0, concat_axis=0)
+    return jnp.concatenate(blocks, axis=along)
 
 
 def along_z(value, shift):
@@ -36,7 +43,7 @@
     facts = jnp.stack([facts] + [along_z(facts, s) for s in range(1, nz)])
     column = jnp.stack([mine] + [along_z(mine, s) for s in range(1, nz)])
     weights = jnp.concatenate([gate_up.reshape(-1, 2 * hid), down_t.reshape(-1, hid)], axis=1)
-    weights = lax.all_gather(weights, "dp", axis=0, tiled=True)
+    weights = exchange_gather(weights, "dp", 0)
     gate_matrix = weights[:, : 2 * hid]
     down_matrix = weights[:, 2 * hid :]
     ids = facts[..., :top].astype(jnp.int32)

time: 334 us -> 424 us (1.27)
  the two profiles are of different devices: /device:TPU:117 before, /device:TPU:85 now
where the time goes in v1:
time: 424 us; the launch traced here: 423 us
  waiting for transfers between devices  288 us (68%)
  starting transfers between devices  90.6 us (21%)
  matrix products  16.5 us (4%)
  local copies, waits for them, and re-layouts  14.9 us (4%)
  other arithmetic  11.3 us (3%)
    all_to_all x1, waiting for transfers between devices, exchange_gather(): blocks = lax.all_to_all(blocks, axis, split_axis=0, concat_axis=0)  97.3 us
    ppermute x9, waiting for transfers between devices, along_z(): lax.ppermute(value, 'z', [(i, (i + shift) % count) for i in range(count)])  80.9 us
    ppermute x9, starting transfers between devices, along_z(): lax.ppermute(value, 'z', [(i, (i + shift) % count) for i in range(count)])  51.4 us
    all_to_all x1, waiting for transfers between devices, local(): rows = lax.all_to_all(rows, PLANE, 0, 0, tiled=True)  46.8 us
    ppermute x1, waiting for transfers between devices, local(): other_down = lax.ppermute(down_t, 'y', pairs)  46.3 us
    all_to_all x1, starting transfers between devices, local(): rows = lax.all_to_all(rows, PLANE, 0, 0, tiled=True)  17.9 us
    all_to_all x1, waiting for transfers between devices, local(): back = lax.all_to_all(back, PLANE, 0, 0, tiled=True)  16.6 us
    all_to_all x1, starting transfers between devices, local(): back = lax.all_to_all(back, PLANE, 0, 0, tiled=True)  9.35 us
  transfers between devices with their start and end apart: 14, of which 9 were waited for; matrix products, arithmetic and copies ran while one was open for 4% of the time, Pallas kernels for 0%

profile of v1, /device:TPU:85, one launch (start us, length us, event | category | flops | bytes accessed | tf_op | source)
XLA Modules:
  0.0 422.8 jit_solution(8788565458360035182)
XLA Ops:
  0.6 1.0 fusion.61
  1.6 10.7 %collective-permute-start.5 = (bf16[2,2,16,2048]{3,2,1,0:T(8,128)(2,1)S(1)}, bf16[2,2,16,2048]{3,2,1,0:T(8,128)(2,1)S(1)}, u32[]{:S(2)}, u32[]{:S(2)}) collective-permute-start(bf16[2,2,16,2048]{3,2,1,0:T(8,128)(2,1)S(1)} %get-tuple-element.16), channel_id=1, source_target_pairs={{0,6},{2,0},{4,2},{6,4},{1,7},{3,1},{5,3},{7,5},{8,14},{10,8},{12,... | collective-permute-start | bytes 786440 | tf_op jit(solution)/shard_map/ppermute | solution.py:21
  12.3 5.2 %collective-permute-start.4 = (bf16[2,2,16,2048]{3,2,1,0:T(8,128)(2,1)S(1)}, bf16[2,2,16,2048]{3,2,1,0:T(8,128)(2,1)S(1)}, u32[]{:S(2)}, u32[]{:S(2)}) collective-permute-start(bf16[2,2,16,2048]{3,2,1,0:T(8,128)(2,1)S(1)} %get-tuple-element.16), channel_id=1, source_target_pairs={{0,4},{2,6},{4,0},{6,2},{1,5},{3,7},{5,1},{7,3},{8,12},{10,14},{12... | collective-permute-start | bytes 786440 | tf_op jit(solution)/shard_map/ppermute | solution.py:21
  17.5 0.7 convert_element_type.77
  18.2 0.7 fusion.60
  18.9 1.9 collective-permute-start.2
  20.8 12.1 %collective-permute-start.1 = (f32[2,16,16]{1,2,0:T(8,128)S(1)}, f32[2,16,16]{1,2,0:T(8,128)S(1)}, u32[]{:S(2)}, u32[]{:S(2)}) collective-permute-start(f32[2,16,16]{1,2,0:T(8,128)S(1)} %get-tuple-element.18), channel_id=1, source_target_pairs={{0,4},{2,6},{4,0},{6,2},{1,5},{3,7},{5,1},{7,3},{8,12},{10,14},{12... | collective-permute-start | bytes 6152 | tf_op jit(solution)/shard_map/ppermute | solution.py:21
  32.9 4.0 collective-permute-start
  36.9 17.7 %collective-permute-done.2 = f32[2,16,16]{1,2,0:T(8,128)S(1)} collective-permute-done((f32[2,16,16]{1,2,0:T(8,128)S(1)}, f32[2,16,16]{1,2,0:T(8,128)S(1)}, u32[]{:S(2)}, u32[]{:S(2)}) %collective-permute-start.2) | collective-permute-done | bytes 2080 | tf_op jit(solution)/shard_map/ppermute | solution.py:21
  54.6 1.9 collective-permute-start.3
  57.8 18.5 %collective-permute-done.3 = bf16[2,2,16,2048]{3,2,1,0:T(8,128)(2,1)S(1)} collective-permute-done((bf16[2,2,16,2048]{3,2,1,0:T(8,128)(2,1)S(1)}, bf16[2,2,16,2048]{3,2,1,0:T(8,128)(2,1)S(1)}, u32[]{:S(2)}, u32[]{:S(2)}) %collective-permute-start.3) | collective-permute-done | bytes 262176 | tf_op jit(solution)/shard_map/ppermute | solution.py:21
  76.4 0.8 convolution_convert_fusion.2
  77.3 0.8 fusion
  78.1 1.2 copy.69
  79.3 1.2 copy.68
  80.4 2.6 pad_maximum_fusion
  83.0 17.9 %all-to-all-start = ((bf16[32,32,2048]{2,1,0:T(8,128)(2,1)}), bf16[32,32,2048]{2,1,0:T(8,128)(2,1)}, u32[]{:S(2)}, u32[]{:S(2)}) async-start(bf16[32,32,2048]{2,1,0:T(8,128)(2,1)} %pad_maximum_fusion), calls=%async_computation | async-start | bytes 8388608 | tf_op jit(solution)/shard_map/all_to_all | solution.py:73
  101.1 46.8 %all-to-all-done = bf16[32,32,2048]{2,1,0:T(8,128)(2,1)} async-done(((bf16[32,32,2048]{2,1,0:T(8,128)(2,1)}), bf16[32,32,2048]{2,1,0:T(8,128)(2,1)}, u32[]{:S(2)}, u32[]{:S(2)}) %all-to-all-start) | async-done | bytes 4194336 | tf_op jit(solution)/shard_map/all_to_all | solution.py:73
  147.9 2.5 stack.68
  150.4 5.1 %all-to-all-start.1 = ((bf16[4,512,1152]{2,1,0:T(8,128)(2,1)}), bf16[4,512,1152]{2,1,0:T(8,128)(2,1)}, u32[]{:S(2)}, u32[]{:S(2)}) async-start(bf16[4,512,1152]{2,1,0:T(8,128)(2,1)} %stack.68), calls=%async_computation.1 | async-start | bytes 9437184 | tf_op jit(solution)/shard_map/all_to_all | solution.py:15
  155.5 4.0 fusion.63
  159.5 97.3 %all-to-all-done.1 = bf16[4,512,1152]{2,1,0:T(8,128)(2,1)} async-done(((bf16[4,512,1152]{2,1,0:T(8,128)(2,1)}), bf16[4,512,1152]{2,1,0:T(8,128)(2,1)}, u32[]{:S(2)}, u32[]{:S(2)}) %all-to-all-start.1) | async-done | bytes 4718624 | tf_op jit(solution)/shard_map/all_to_all | solution.py:15
  256.8 3.7 fusion.2
  260.5 2.9 convolution_convert_fusion.1
  263.4 2.9 multiply_convert_fusion.1
  266.2 3.7 convolution_convert_fusion
  269.9 2.6 pad_maximum_fusion.1
  272.5 9.3 %all-to-all-start.2 = ((bf16[32,32,2048]{2,1,0:T(8,128)(2,1)}), bf16[32,32,2048]{2,1,0:T(8,128)(2,1)}, u32[]{:S(2)}, u32[]{:S(2)}) async-start(bf16[32,32,2048]{2,1,0:T(8,128)(2,1)} %pad_maximum_fusion.1), calls=%async_computation.2 | async-start | bytes 8388608 | tf_op jit(solution)/shard_map/all_to_all | solution.py:91
  281.9 2.2 collective-permute-start.10
  284.1 4.6 %collective-permute-start.9 = (bf16[1,512,2,384]{3,2,1,0:T(2,128)(2,1)S(1)}, bf16[1,512,2,384]{3,2,1,0:T(2,128)(2,1)S(1)}, u32[]{:S(2)}, u32[]{:S(2)}) collective-permute-start(bf16[1,512,2,384]{3,2,1,0:T(2,128)(2,1)S(1)} %copy-done), channel_id=1, source_target_pairs={{0,64},{32,96},{64,0},{96,32},{1,65},{33,97},{65,1},{97,33},{2,66}... | collective-permute-start | bytes 2359304 | tf_op jit(solution)/shard_map/ppermute | solution.py:37
  288.7 0.6 fusion.53
  290.0 46.3 %collective-permute-done.10 = bf16[1,512,384]{2,1,0:T(8,128)(2,1)S(1)} collective-permute-done((bf16[1,512,384]{2,1,0:T(8,128)(2,1)S(1)}, bf16[1,512,384]{2,1,0:T(8,128)(2,1)S(1)}, u32[]{:S(2)}, u32[]{:S(2)}) %collective-permute-start.10) | collective-permute-done | bytes 393248 | tf_op jit(solution)/shard_map/ppermute | solution.py:38
  336.3 0.8 broadcast_select_fusion.1
  337.1 16.6 %all-to-all-done.2 = bf16[32,32,2048]{2,1,0:T(8,128)(2,1)} async-done(((bf16[32,32,2048]{2,1,0:T(8,128)(2,1)}), bf16[32,32,2048]{2,1,0:T(8,128)(2,1)}, u32[]{:S(2)}, u32[]{:S(2)}) %all-to-all-start.2) | async-done | bytes 4194336 | tf_op jit(solution)/shard_map/all_to_all | solution.py:91
  353.7 2.7 fusion.62
  356.4 1.2 copy.95
  357.6 0.5 convolution_bitcast_fusion.2
  358.1 1.2 copy.96
  359.3 0.5 convolution_bitcast_fusion
  359.8 0.5 fusion.5
  360.6 1.9 collective-permute-start.8
  362.5 9.4 %collective-permute-start.7 = (bf16[2,2,16,2048]{3,2,1,0:T(8,128)(2,1)S(1)}, bf16[2,2,16,2048]{3,2,1,0:T(8,128)(2,1)S(1)}, u32[]{:S(2)}, u32[]{:S(2)}) collective-permute-start(bf16[2,2,16,2048]{3,2,1,0:T(8,128)(2,1)S(1)} %get-tuple-element.12), channel_id=1, source_target_pairs={{0,4},{2,6},{4,0},{6,2},{1,5},{3,7},{5,1},{7,3},{8,12},{10,14},{12... | collective-permute-start | bytes 786440 | tf_op jit(solution)/shard_map/ppermute | solution.py:21
  372.0 4.3 %collective-permute-start.6 = (bf16[2,2,16,2048]{3,2,1,0:T(8,128)(2,1)S(1)}, bf16[2,2,16,2048]{3,2,1,0:T(8,128)(2,1)S(1)}, u32[]{:S(2)}, u32[]{:S(2)}) collective-permute-start(bf16[2,2,16,2048]{3,2,1,0:T(8,128)(2,1)S(1)} %get-tuple-element.10), channel_id=1, source_target_pairs={{0,6},{2,0},{4,2},{6,4},{1,7},{3,1},{5,3},{7,5},{8,14},{10,8},{12,... | collective-permute-start | bytes 786440 | tf_op jit(solution)/shard_map/ppermute | solution.py:21
  376.3 1.0 broadcast_select_fusion
  377.3 5.3 %collective-permute-done.8 = bf16[2,2,16,2048]{3,2,1,0:T(8,128)(2,1)S(1)} collective-permute-done((bf16[2,2,16,2048]{3,2,1,0:T(8,128)(2,1)S(1)}, bf16[2,2,16,2048]{3,2,1,0:T(8,128)(2,1)S(1)}, u32[]{:S(2)}, u32[]{:S(2)}) %collective-permute-start.8) | collective-permute-done | bytes 262176 | tf_op jit(solution)/shard_map/ppermute | solution.py:21
  382.6 10.0 %collective-permute-done.7 = bf16[2,2,16,2048]{3,2,1,0:T(8,128)(2,1)S(1)} collective-permute-done((bf16[2,2,16,2048]{3,2,1,0:T(8,128)(2,1)S(1)}, bf16[2,2,16,2048]{3,2,1,0:T(8,128)(2,1)S(1)}, u32[]{:S(2)}, u32[]{:S(2)}) %collective-permute-start.7) | collective-permute-done | bytes 262176 | tf_op jit(solution)/shard_map/ppermute | solution.py:21
  392.7 29.3 %collective-permute-done.6 = bf16[2,2,16,2048]{3,2,1,0:T(8,128)(2,1)S(1)} collective-permute-done((bf16[2,2,16,2048]{3,2,1,0:T(8,128)(2,1)S(1)}, bf16[2,2,16,2048]{3,2,1,0:T(8,128)(2,1)S(1)}, u32[]{:S(2)}, u32[]{:S(2)}) %collective-permute-start.6) | collective-permute-done | bytes 262176 | tf_op jit(solution)/shard_map/ppermute | solution.py:21
  422.1 0.7 slice_bitcast_fusion.7
  (30 shorter events, 1.9 us)
Async XLA Ops:
  1.6 56.1 %collective-permute-start.5 = (bf16[2,2,16,2048]{3,2,1,0:T(8,128)(2,1)S(1)}, bf16[2,2,16,2048]{3,2,1,0:T(8,128)(2,1)S(1)}, u32[]{:S(2)}, u32[]{:S(2)}) collective-permute-start(bf16[2,2,16,2048]{3,2,1,0:T(8,128)(2,1)S(1)} %get-tuple-element.16), channel_id=1, source_target_pairs={{0,6},{2,0},{4,2},{6,4},{1,7},{3,1},{5,3},{7,5},{8,14},{10,8},{12,... | collective-permute-start | bytes 786440 | tf_op jit(solution)/shard_map/ppermute | solution.py:21
  12.3 45.5 %collective-permute-start.4 = (bf16[2,2,16,2048]{3,2,1,0:T(8,128)(2,1)S(1)}, bf16[2,2,16,2048]{3,2,1,0:T(8,128)(2,1)S(1)}, u32[]{:S(2)}, u32[]{:S(2)}) collective-permute-start(bf16[2,2,16,2048]{3,2,1,0:T(8,128)(2,1)S(1)} %get-tuple-element.16), channel_id=1, source_target_pairs={{0,4},{2,6},{4,0},{6,2},{1,5},{3,7},{5,1},{7,3},{8,12},{10,14},{12... | collective-permute-start | bytes 786440 | tf_op jit(solution)/shard_map/ppermute | solution.py:21
  18.9 35.8 %collective-permute-start.2 = (f32[2,16,16]{1,2,0:T(8,128)S(1)}, f32[2,16,16]{1,2,0:T(8,128)S(1)}, u32[]{:S(2)}, u32[]{:S(2)}) collective-permute-start(f32[2,16,16]{1,2,0:T(8,128)S(1)} %get-tuple-element.18), channel_id=1, source_target_pairs={{0,6},{2,0},{4,2},{6,4},{1,7},{3,1},{5,3},{7,5},{8,14},{10,8},{12,... | collective-permute-start | bytes 6152 | tf_op jit(solution)/shard_map/ppermute | solution.py:21
  20.8 35.8 %collective-permute-start.1 = (f32[2,16,16]{1,2,0:T(8,128)S(1)}, f32[2,16,16]{1,2,0:T(8,128)S(1)}, u32[]{:S(2)}, u32[]{:S(2)}) collective-permute-start(f32[2,16,16]{1,2,0:T(8,128)S(1)} %get-tuple-element.18), channel_id=1, source_target_pairs={{0,4},{2,6},{4,0},{6,2},{1,5},{3,7},{5,1},{7,3},{8,12},{10,14},{12... | collective-permute-start | bytes 6152 | tf_op jit(solution)/shard_map/ppermute | solution.py:21
  32.9 23.7 %collective-permute-start = (f32[2,16,16]{1,2,0:T(8,128)S(1)}, f32[2,16,16]{1,2,0:T(8,128)S(1)}, u32[]{:S(2)}, u32[]{:S(2)}) collective-permute-start(f32[2,16,16]{1,2,0:T(8,128)S(1)} %get-tuple-element.18), channel_id=1, source_target_pairs={{0,2},{2,4},{4,6},{6,0},{1,3},{3,5},{5,7},{7,1},{8,10},{10,12},{12... | collective-permute-start | bytes 6152 | tf_op jit(solution)/shard_map/ppermute | solution.py:21
  54.6 21.7 %collective-permute-start.3 = (bf16[2,2,16,2048]{3,2,1,0:T(8,128)(2,1)S(1)}, bf16[2,2,16,2048]{3,2,1,0:T(8,128)(2,1)S(1)}, u32[]{:S(2)}, u32[]{:S(2)}) collective-permute-start(bf16[2,2,16,2048]{3,2,1,0:T(8,128)(2,1)S(1)} %get-tuple-element.16), channel_id=1, source_target_pairs={{0,2},{2,4},{4,6},{6,0},{1,3},{3,5},{5,7},{7,1},{8,10},{10,12},{12... | collective-permute-start | bytes 786440 | tf_op jit(solution)/shard_map/ppermute | solution.py:21
  83.0 17.9 %copy-start = (bf16[1,512,2,384]{3,2,1,0:T(2,128)(2,1)S(1)}, bf16[1,512,2,384]{3,2,1,0:T(2,128)(2,1)}, u32[]{:S(2)}) copy-start(bf16[1,512,2,384]{3,2,1,0:T(2,128)(2,1)} %param.12) | copy-start | bytes 2359300
  83.0 18.0 %copy-start.2 = (bf16[1,512,384]{2,1,0:T(8,128)(2,1)S(1)}, bf16[1,512,384]{2,1,0:T(8,128)(2,1)}, u32[]{:S(2)}) copy-start(bf16[1,512,384]{2,1,0:T(8,128)(2,1)} %param.13) | copy-start | bytes 1179652
  83.0 64.9 %all-to-all-start = ((bf16[32,32,2048]{2,1,0:T(8,128)(2,1)}), bf16[32,32,2048]{2,1,0:T(8,128)(2,1)}, u32[]{:S(2)}, u32[]{:S(2)}) async-start(bf16[32,32,2048]{2,1,0:T(8,128)(2,1)} %pad_maximum_fusion), calls=%async_computation | async-start | bytes 8388608 | tf_op jit(solution)/shard_map/all_to_all | solution.py:73
  150.4 106.4 %all-to-all-start.1 = ((bf16[4,512,1152]{2,1,0:T(8,128)(2,1)}), bf16[4,512,1152]{2,1,0:T(8,128)(2,1)}, u32[]{:S(2)}, u32[]{:S(2)}) async-start(bf16[4,512,1152]{2,1,0:T(8,128)(2,1)} %stack.68), calls=%async_computation.1 | async-start | bytes 9437184 | tf_op jit(solution)/shard_map/all_to_all | solution.py:15
  260.5 2.9 copy-start.1
  272.5 16.2 %copy-start.3 = (s32[64]{0:T(128)S(1)}, s32[64]{0:T(128)}, u32[]{:S(2)}) copy-start(s32[64]{0:T(128)} %param.11) | copy-start | bytes 772
  272.5 81.2 %all-to-all-start.2 = ((bf16[32,32,2048]{2,1,0:T(8,128)(2,1)}), bf16[32,32,2048]{2,1,0:T(8,128)(2,1)}, u32[]{:S(2)}, u32[]{:S(2)}) async-start(bf16[32,32,2048]{2,1,0:T(8,128)(2,1)} %pad_maximum_fusion.1), calls=%async_computation.2 | async-start | bytes 8388608 | tf_op jit(solution)/shard_map/all_to_all | solution.py:91
  281.9 54.5 %collective-permute-start.10 = (bf16[1,512,384]{2,1,0:T(8,128)(2,1)S(1)}, bf16[1,512,384]{2,1,0:T(8,128)(2,1)S(1)}, u32[]{:S(2)}, u32[]{:S(2)}) collective-permute-start(bf16[1,512,384]{2,1,0:T(8,128)(2,1)S(1)} %copy-done.2), channel_id=1, source_target_pairs={{0,64},{32,96},{64,0},{96,32},{1,65},{33,97},{65,1},{97,33},{2,66}... | collective-permute-start | bytes 1179656 | tf_op jit(solution)/shard_map/ppermute | solution.py:38
  284.1 92.3 %collective-permute-start.9 = (bf16[1,512,2,384]{3,2,1,0:T(2,128)(2,1)S(1)}, bf16[1,512,2,384]{3,2,1,0:T(2,128)(2,1)S(1)}, u32[]{:S(2)}, u32[]{:S(2)}) collective-permute-start(bf16[1,512,2,384]{3,2,1,0:T(2,128)(2,1)S(1)} %copy-done), channel_id=1, source_target_pairs={{0,64},{32,96},{64,0},{96,32},{1,65},{33,97},{65,1},{97,33},{2,66}... | collective-permute-start | bytes 2359304 | tf_op jit(solution)/shard_map/ppermute | solution.py:37
  360.6 22.1 %collective-permute-start.8 = (bf16[2,2,16,2048]{3,2,1,0:T(8,128)(2,1)S(1)}, bf16[2,2,16,2048]{3,2,1,0:T(8,128)(2,1)S(1)}, u32[]{:S(2)}, u32[]{:S(2)}) collective-permute-start(bf16[2,2,16,2048]{3,2,1,0:T(8,128)(2,1)S(1)} %get-tuple-element.11), channel_id=1, source_target_pairs={{0,2},{2,4},{4,6},{6,0},{1,3},{3,5},{5,7},{7,1},{8,10},{10,12},{12... | collective-permute-start | bytes 786440 | tf_op jit(solution)/shard_map/ppermute | solution.py:21
  362.5 30.2 %collective-permute-start.7 = (bf16[2,2,16,2048]{3,2,1,0:T(8,128)(2,1)S(1)}, bf16[2,2,16,2048]{3,2,1,0:T(8,128)(2,1)S(1)}, u32[]{:S(2)}, u32[]{:S(2)}) collective-permute-start(bf16[2,2,16,2048]{3,2,1,0:T(8,128)(2,1)S(1)} %get-tuple-element.12), channel_id=1, source_target_pairs={{0,4},{2,6},{4,0},{6,2},{1,5},{3,7},{5,1},{7,3},{8,12},{10,14},{12... | collective-permute-start | bytes 786440 | tf_op jit(solution)/shard_map/ppermute | solution.py:21
  372.0 50.0 %collective-permute-start.6 = (bf16[2,2,16,2048]{3,2,1,0:T(8,128)(2,1)S(1)}, bf16[2,2,16,2048]{3,2,1,0:T(8,128)(2,1)S(1)}, u32[]{:S(2)}, u32[]{:S(2)}) collective-permute-start(bf16[2,2,16,2048]{3,2,1,0:T(8,128)(2,1)S(1)} %get-tuple-element.10), channel_id=1, source_target_pairs={{0,6},{2,0},{4,2},{6,4},{1,7},{3,1},{5,3},{7,5},{8,14},{10,8},{12,... | collective-permute-start | bytes 786440 | tf_op jit(solution)/shard_map/ppermute | solution.py:21
